TPU v7x, 32 devices: a whole 2x2x4 slice. The times are simulated.
32 devices in a mesh: group: 4 (over x, core), dev: 8 (over z, y).
Axes of the slice: x: 2, y: 2, z: 4, core: 2. Of those that a mesh axis runs over, the one named last changes fastest.
Arguments:
- elem_ops: bfloat16 [2048, 48, 64], P(('group', 'dev')), may hold values from -0.75 to 0.75
- elem_stiff: bfloat16 [2048, 48], P(('group', 'dev')), may hold values from 0.5 to 4
- owner: int32 [2048, 1], P(('group', 'dev')), may hold values from 0 to 7; in each aligned block of 64 rows (0 to 63, 64 to 127, ...) at most 16 rows name the same one
- row_slot: int32 [2048], P(('group', 'dev')), may hold values from 0 to 63
- couplings: float32 [2048, 4, 64, 64], P(('group', 'dev')), may hold values from -0.12 to 0.12
- coupling_cols: int32 [2048, 4], P(('group', 'dev')), may hold values from 0 to 191, as said below
- mass: float32 [2048, 64], P(('group', 'dev')), may hold values from 2 to 4
- rhs: float32 [2048, 64], P(('group', 'dev')), may hold values from -48 to 48
Outputs:
- solution: float32 [2048, 64], P(('group', 'dev'))
- residual: float32 [2048, 64], P(('group', 'dev'))
Inputs may be any that keep to these rules, and one draw needn't show every extreme that they name: Among the 64 elements of one device (each aligned block of 64 entries) no owner is named more than 16 times, a bound that some block reaches. `coupling_cols`: A value below 64 names a block row of the lower lateral group, one below 128 the device's own, the rest the upper lateral group, as in the operator's step.
All inputs are finite; a program needn't handle non-finite values.
Results may differ from a plain program's by a relative error of at most 0.0005.
Values may be sent and summed in bfloat16 or wider, within the bound.
A program may use at most 64 MiB of HBM per device.

v0:
```python
import jax
import jax.numpy as jnp
from jax import lax
from jax.sharding import PartitionSpec as P

BS = 64
K = 4
ITERS = 3


def padded(shard, sides, width):
    for axis, dim in sides:
        count, length = (lax.axis_size(axis), shard.shape[dim])
        up = [(i, (i + 1) % count) for i in range(count - 1)]
        down = [(j, i) for i, j in up]
        last = lax.slice_in_dim(shard, length - width, length, axis=dim)
        first = lax.slice_in_dim(shard, 0, width, axis=dim)
        before = lax.ppermute(last, axis, up)
        after = lax.ppermute(first, axis, down)
        shard = jnp.concatenate([before, shard, after], axis=dim)
    return shard


def shifted(shard, axis, by):
    count = lax.axis_size(axis)
    pairs = [(i, i + by) for i in range(count) if 0 <= i + by < count]
    return lax.ppermute(shard, axis, pairs)


def element_tangents(element_ops, element_stiff):
    values = element_ops.astype(jnp.float32)
    weights = element_stiff.astype(jnp.float32)
    return jnp.einsum("eqi,eq,eqj->eij", values, weights, values, precision=lax.Precision.HIGHEST)


def per_device(elem_ops, elem_stiff, owner, row_slot, couplings, coupling_cols, mass, rhs):
    rows_here = rhs.shape[0]
    owners = lax.axis_size("dev")
    count = elem_ops.shape[0]
    capacity = 2 * count // owners
    slots = owners * capacity
    target = owner[:, 0]
    member = (target[:, None] == jnp.arange(owners, dtype=jnp.int32)[None, :]).astype(jnp.int32)
    before = jnp.cumsum(member, axis=0) - member
    position = target * capacity + jnp.sum(before * member, axis=1)
    row_buffer = (
        jnp.full((slots,), -1, jnp.int32).at[position].set(row_slot).reshape(owners, capacity)
    )
    local_tangent = element_tangents(elem_ops, elem_stiff).reshape(count, BS * BS)
    tangent_buffer = jnp.zeros((slots, BS * BS), jnp.float32).at[position].set(local_tangent)
    tangent_buffer = tangent_buffer.reshape(owners, capacity, BS * BS)
    tangent, got_rows = (
        lax.all_to_all(tangent_buffer, "dev", split_axis=0, concat_axis=0, tiled=True),
        lax.all_to_all(row_buffer, "dev", split_axis=0, concat_axis=0, tiled=True),
    )
    tangent = tangent.reshape(slots, BS * BS)
    got_rows = got_rows.reshape(slots)
    selector = (got_rows[None, :] == jnp.arange(rows_here, dtype=jnp.int32)[:, None]).astype(
        jnp.float32
    )
    diag_block = jnp.dot(selector, tangent, precision=lax.Precision.HIGHEST).reshape(
        rows_here, BS, BS
    )
    flat_cols = coupling_cols.reshape(-1)
    placer = (flat_cols[None, :] == jnp.arange(3 * rows_here, dtype=jnp.int32)[:, None]).astype(
        jnp.float32
    )

    def apply_operator(field):
        extended = padded(field.reshape(1, rows_here, BS), (("group", 0),), 1)
        extended = extended.reshape(3 * rows_here, BS)
        nearby = jnp.take(extended, flat_cols, axis=0).reshape(rows_here, K, BS)
        own_part = jnp.einsum("rij,rj->ri", diag_block, field, precision=lax.Precision.HIGHEST)
        cross = jnp.einsum("rkij,rkj->ri", couplings, nearby, precision=lax.Precision.HIGHEST)
        returned = jnp.einsum("rkij,ri->rkj", couplings, field, precision=lax.Precision.HIGHEST)
        spread = jnp.dot(
            placer, returned.reshape(rows_here * K, BS), precision=lax.Precision.HIGHEST
        )
        spread = spread.reshape(3, rows_here, BS)
        from_upper = shifted(spread[0], "group", -1)
        from_lower = shifted(spread[2], "group", 1)
        return own_part + mass * field + cross + spread[1] + from_upper + from_lower

    solution = jnp.zeros_like(rhs)
    residual = rhs

    def paired_sums(current, product_image):
        return lax.psum(
            (jnp.sum(current * current), jnp.sum(current * product_image)), ("group", "dev")
        )

    image = apply_operator(residual)
    norm_now, product = paired_sums(residual, image)
    alpha = norm_now / product
    direction = residual
    along = image
    for iteration in range(ITERS):
        solution = solution + alpha * direction
        residual = residual - alpha * along
        if iteration + 1 < ITERS:
            image = apply_operator(residual)
            norm_next, product = paired_sums(residual, image)
            ratio = norm_next / norm_now
            alpha = norm_next / (product - ratio * norm_next / alpha)
            direction = residual + ratio * direction
            along = image + ratio * along
            norm_now = norm_next
    return (solution, residual)


def solution(mesh):
    placed = (
        P(("group", "dev"), None, None),
        P(("group", "dev"), None),
        P(("group", "dev"), None),
        P(("group", "dev")),
        P(("group", "dev"), None, None, None),
        P(("group", "dev"), None),
        P(("group", "dev"), None),
        P(("group", "dev"), None),
    )
    return jax.shard_map(
        per_device,
        mesh=mesh,
        in_specs=placed,
        out_specs=(P(("group", "dev"), None), P(("group", "dev"), None)),
        check_vma=False,
    )
```

profile of v0, /device:TPU:0, one launch (start us, length us, event | category | flops | bytes accessed | tf_op | source)
XLA Modules:
  0.0 276.3 jit_solution(9372823602947593937)
XLA Ops:
  4.5 7.3 %all-to-all-start = ((s32[8,1,16]{2,1,0:T(1,128)}), s32[8,1,16]{2,1,0:T(1,128)S(1)}, u32[]{:S(2)}, u32[]{:S(2)}) async-start(s32[8,1,16]{2,1,0:T(1,128)} %bitcast.5), calls=%async_computation | async-start | bytes 8192 | tf_op jit(solution)/shard_map/all_to_all | solution.py:54
  12.6 3.7 %convolution_bitcast_fusion = f32[64,64,64]{1,2,0:T(8,128)S(1)} fusion(bf16[64,48,64]{2,1,0:T(8,128)(2,1)} %param.10, f32[64,48]{1,0:T(8,128)S(1)} %copy.38), kind=kOutput, calls=%fused_computation.9 | convolution fusion | flops 151388160 | bytes 1454080 | tf_op jit(solution)/shard_map/eqi,eq,eqj->eij/dot_general | solution.py:33
  16.3 1.9 copy.39
  18.2 2.1 reshape.140
  20.3 2.6 scatter_custom_fusion.1
  22.9 6.1 %all-to-all-start.1 = ((f32[8,16,4096]{2,1,0:T(8,128)}), f32[8,16,4096]{2,1,0:T(8,128)S(1)}, u32[]{:S(2)}, u32[]{:S(2)}) async-start(f32[8,16,4096]{2,1,0:T(8,128)} %bitcast.8), calls=%async_computation.1 | async-start | bytes 4194304 | tf_op jit(solution)/shard_map/all_to_all | solution.py:53
  30.4 1.3 collective-permute-start.1
  31.9 6.8 %fusion.34 = f32[64,1,4,64]{3,1,2,0:T(1,128)S(1)} fusion(f32[64,4,64,64]{3,2,1,0:T(8,128)} %param.14, f32[64,64,1,1]{1,2,3,0:T(1,128)S(1)} %bitcast.116), kind=kOutput, calls=%fused_computation.71 | convolution fusion | flops 12582912 | bytes 4276224 | tf_op jit(solution)/shard_map/rkij,ri->rkj/dot_general | solution.py:75
  40.3 5.6 %collective-permute-start.3 = (f32[64,64]{0,1:T(8,128)S(1)}, f32[64,64]{0,1:T(8,128)S(1)}, u32[]{:S(2)}, u32[]{:S(2)}) collective-permute-start(f32[64,64]{0,1:T(8,128)S(1)} %get-tuple-element.28), channel_id=1, source_target_pairs={{0,8},{8,16},{16,24},{1,9},{9,17},{17,25},{2,10},{10,18},{18,26},{... | collective-permute-start | bytes 49160 | tf_op jit(solution)/shard_map/ppermute | solution.py:27
  48.8 9.0 %fusion.33 = f32[64,1,64,1]{2,1,3,0:T(1,128)S(1)} fusion(f32[64,4,64,1]{2,3,1,0:T(1,128)S(1)} %bitcast.121, f32[64,4,64,64]{3,2,1,0:T(8,128)} %param.14), kind=kOutput, calls=%fused_computation.70 | convolution fusion | flops 12582912 | bytes 4276224 | tf_op jit(solution)/shard_map/rkij,rkj->ri/dot_general | solution.py:74
  57.9 18.9 %all-to-all-done.1 = f32[8,16,4096]{2,1,0:T(8,128)S(1)} async-done(((f32[8,16,4096]{2,1,0:T(8,128)}), f32[8,16,4096]{2,1,0:T(8,128)S(1)}, u32[]{:S(2)}, u32[]{:S(2)}) %all-to-all-start.1) | async-done | bytes 2097184 | tf_op jit(solution)/shard_map/all_to_all | solution.py:53
  76.7 1.9 copy.40
  78.6 4.7 %fusion.21 = f32[64,64,64]{2,0,1:T(8,128)S(1)} fusion(f32[64,64,128]{2,1,0:T(8,128)} %bitcast.105, s32[128]{0:T(128)S(1)} %eq.47), kind=kOutput, calls=%fused_computation.57 | convolution fusion | flops 402661376 | bytes 3146240 | tf_op jit(solution)/shard_map/dot_general | solution.py:61
  83.3 4.5 %fusion = f32[64,1,64]{2,1,0:T(1,128)S(1)} fusion(f32[64,64,1]{1,2,0:T(1,128)S(1)} %bitcast.118, f32[64,64,64]{2,0,1:T(8,128)S(1)} %fusion.21), kind=kOutput, calls=%fused_computation.7 | convolution fusion | flops 3145728 | bytes 1081344 | tf_op jit(solution)/shard_map/rij,rj->ri/dot_general | solution.py:73
  88.6 38.0 %all-reduce.2 = (f32[]{:T(128)}, f32[]{:T(128)}) all-reduce(f32[]{:T(128)} %multiply_reduce_fusion.7, f32[]{:T(128)} %get-tuple-element.21), channel_id=1, replica_groups=mesh['group'=4,'dev'=8] {'group','dev'}, use_global_device_ids=true, to_apply=%region_1.2 | all-reduce | flops 2 | bytes 16 | tf_op jit(solution)/shard_map/psum | solution.py:88
  129.3 1.5 collective-permute-start.5
  130.9 6.4 %fusion.36 = f32[64,1,4,64]{3,1,2,0:T(1,128)S(1)} fusion(f32[64,64,1,1]{1,2,3,0:T(1,128)S(1)} %copy.67, f32[64,4,64,64]{3,2,1,0:T(8,128)} %param.14), kind=kOutput, calls=%fused_computation.73 | convolution fusion | flops 12582912 | bytes 4276224 | tf_op jit(solution)/shard_map/rkij,ri->rkj/dot_general | solution.py:75
  139.5 6.2 %collective-permute-start.7 = (f32[64,64]{0,1:T(8,128)S(1)}, f32[64,64]{0,1:T(8,128)S(1)}, u32[]{:S(2)}, u32[]{:S(2)}) collective-permute-start(f32[64,64]{0,1:T(8,128)S(1)} %get-tuple-element.26), channel_id=1, source_target_pairs={{0,8},{8,16},{16,24},{1,9},{9,17},{17,25},{2,10},{10,18},{18,26},{... | collective-permute-start | bytes 49160 | tf_op jit(solution)/shard_map/ppermute | solution.py:27
  146.7 9.0 %fusion.35 = f32[64,1,64,1]{2,1,3,0:T(1,128)S(1)} fusion(f32[64,4,64,1]{2,3,1,0:T(1,128)S(1)} %bitcast.123, f32[64,4,64,64]{3,2,1,0:T(8,128)} %param.14), kind=kOutput, calls=%fused_computation.72 | convolution fusion | flops 12582912 | bytes 4276224 | tf_op jit(solution)/shard_map/rkij,rkj->ri/dot_general | solution.py:74
  156.6 41.7 %all-reduce.1 = (f32[]{:T(128)}, f32[]{:T(128)}) all-reduce(f32[]{:T(128)} %get-tuple-element.12, f32[]{:T(128)} %get-tuple-element.11), channel_id=1, replica_groups=mesh['group'=4,'dev'=8] {'group','dev'}, use_global_device_ids=true, to_apply=%region_9.11 | all-reduce | flops 2 | bytes 16 | tf_op jit(solution)/shard_map/psum | solution.py:88
  205.6 6.4 %fusion.38 = f32[64,1,4,64]{3,1,2,0:T(1,128)S(1)} fusion(f32[64,64,1,1]{1,2,3,0:T(1,128)S(1)} %copy.75, f32[64,4,64,64]{3,2,1,0:T(8,128)} %param.14), kind=kOutput, calls=%fused_computation.75 | convolution fusion | flops 12582912 | bytes 4276224 | tf_op jit(solution)/shard_map/rkij,ri->rkj/dot_general | solution.py:75
  214.2 6.4 %collective-permute-start.11 = (f32[64,64]{0,1:T(8,128)S(1)}, f32[64,64]{0,1:T(8,128)S(1)}, u32[]{:S(2)}, u32[]{:S(2)}) collective-permute-start(f32[64,64]{0,1:T(8,128)S(1)} %get-tuple-element.24), channel_id=1, source_target_pairs={{0,8},{8,16},{16,24},{1,9},{9,17},{17,25},{2,10},{10,18},{18,26},{... | collective-permute-start | bytes 49160 | tf_op jit(solution)/shard_map/ppermute | solution.py:27
  221.6 9.0 %fusion.37 = f32[64,1,64,1]{2,1,3,0:T(1,128)S(1)} fusion(f32[64,4,64,1]{2,3,1,0:T(1,128)S(1)} %bitcast.120, f32[64,4,64,64]{3,2,1,0:T(8,128)} %param.14), kind=kOutput, calls=%fused_computation.74 | convolution fusion | flops 12582912 | bytes 4276224 | tf_op jit(solution)/shard_map/rkij,rkj->ri/dot_general | solution.py:74
  231.5 39.5 %all-reduce = (f32[]{:T(128)}, f32[]{:T(128)}) all-reduce(f32[]{:T(128)} %get-tuple-element.10, f32[]{:T(128)} %get-tuple-element.9), channel_id=1, replica_groups=mesh['group'=4,'dev'=8] {'group','dev'}, use_global_device_ids=true, to_apply=%region_13.15 | all-reduce | flops 2 | bytes 16 | tf_op jit(solution)/shard_map/psum | solution.py:88
  (79 shorter events, 25.0 us)
Async XLA Ops:
  4.5 18.4 %all-to-all-start = ((s32[8,1,16]{2,1,0:T(1,128)}), s32[8,1,16]{2,1,0:T(1,128)S(1)}, u32[]{:S(2)}, u32[]{:S(2)}) async-start(s32[8,1,16]{2,1,0:T(1,128)} %bitcast.5), calls=%async_computation | async-start | bytes 8192 | tf_op jit(solution)/shard_map/all_to_all | solution.py:54
  22.9 6.1 %copy-start = (f32[64,64]{1,0:T(8,128)S(1)}, f32[64,64]{1,0:T(8,128)}, u32[]{:S(2)}) copy-start(f32[64,64]{1,0:T(8,128)} %param.17) | copy-start | bytes 49156
  22.9 8.7 %copy-start.2 = (s32[64,4]{0,1:T(4,128)S(1)}, s32[64,4]{0,1:T(4,128)}, u32[]{:S(2)}) copy-start(s32[64,4]{0,1:T(4,128)} %param.15) | copy-start | bytes 3076
  22.9 53.8 %all-to-all-start.1 = ((f32[8,16,4096]{2,1,0:T(8,128)}), f32[8,16,4096]{2,1,0:T(8,128)S(1)}, u32[]{:S(2)}, u32[]{:S(2)}) async-start(f32[8,16,4096]{2,1,0:T(8,128)} %bitcast.8), calls=%async_computation.1 | async-start | bytes 4194304 | tf_op jit(solution)/shard_map/all_to_all | solution.py:53
  29.1 18.8 %collective-permute-start = (f32[1,64,64]{2,1,0:T(8,128)S(1)}, f32[1,64,64]{2,1,0:T(8,128)S(1)}, u32[]{:S(2)}, u32[]{:S(2)}) collective-permute-start(f32[1,64,64]{2,1,0:T(8,128)S(1)} %bitcast.114), channel_id=1, source_target_pairs={{0,8},{8,16},{16,24},{1,9},{9,17},{17,25},{2,10},{10,18},{18,26},{... | collective-permute-start | bytes 49160 | tf_op jit(solution)/shard_map/ppermute | solution.py:18
  30.4 17.5 %collective-permute-start.1 = (f32[1,64,64]{2,1,0:T(8,128)S(1)}, f32[1,64,64]{2,1,0:T(8,128)S(1)}, u32[]{:S(2)}, u32[]{:S(2)}) collective-permute-start(f32[1,64,64]{2,1,0:T(8,128)S(1)} %bitcast.115), channel_id=1, source_target_pairs={{8,0},{16,8},{24,16},{9,1},{17,9},{25,17},{10,2},{18,10},{26,18},{... | collective-permute-start | bytes 49160 | tf_op jit(solution)/shard_map/ppermute | solution.py:19
  31.9 14.7 %copy-start.1 = (f32[64,64]{1,0:T(8,128)S(1)}, f32[64,64]{1,0:T(8,128)}, u32[]{:S(2)}) copy-start(f32[64,64]{1,0:T(8,128)} %param.16) | copy-start | bytes 49156
  39.0 48.9 %collective-permute-start.2 = (f32[64,64]{0,1:T(8,128)S(1)}, f32[64,64]{0,1:T(8,128)S(1)}, u32[]{:S(2)}, u32[]{:S(2)}) collective-permute-start(f32[64,64]{0,1:T(8,128)S(1)} %get-tuple-element.27), channel_id=1, source_target_pairs={{8,0},{16,8},{24,16},{9,1},{17,9},{25,17},{10,2},{18,10},{26,18},{... | collective-permute-start | bytes 49160 | tf_op jit(solution)/shard_map/ppermute | solution.py:27
  40.3 47.6 %collective-permute-start.3 = (f32[64,64]{0,1:T(8,128)S(1)}, f32[64,64]{0,1:T(8,128)S(1)}, u32[]{:S(2)}, u32[]{:S(2)}) collective-permute-start(f32[64,64]{0,1:T(8,128)S(1)} %get-tuple-element.28), channel_id=1, source_target_pairs={{0,8},{8,16},{16,24},{1,9},{9,17},{17,25},{2,10},{10,18},{18,26},{... | collective-permute-start | bytes 49160 | tf_op jit(solution)/shard_map/ppermute | solution.py:27
  128.0 17.7 %collective-permute-start.4 = (f32[1,64,64]{1,2,0:T(8,128)S(1)}, f32[1,64,64]{1,2,0:T(8,128)S(1)}, u32[]{:S(2)}, u32[]{:S(2)}) collective-permute-start(f32[1,64,64]{1,2,0:T(8,128)S(1)} %bitcast.106), channel_id=1, source_target_pairs={{0,8},{8,16},{16,24},{1,9},{9,17},{17,25},{2,10},{10,18},{18,26},{... | collective-permute-start | bytes 49160 | tf_op jit(solution)/shard_map/ppermute | solution.py:18
  129.3 16.4 %collective-permute-start.5 = (f32[1,64,64]{1,2,0:T(8,128)S(1)}, f32[1,64,64]{1,2,0:T(8,128)S(1)}, u32[]{:S(2)}, u32[]{:S(2)}) collective-permute-start(f32[1,64,64]{1,2,0:T(8,128)S(1)} %bitcast.107), channel_id=1, source_target_pairs={{8,0},{16,8},{24,16},{9,1},{17,9},{25,17},{10,2},{18,10},{26,18},{... | collective-permute-start | bytes 49160 | tf_op jit(solution)/shard_map/ppermute | solution.py:19
  138.2 17.6 %collective-permute-start.6 = (f32[64,64]{0,1:T(8,128)S(1)}, f32[64,64]{0,1:T(8,128)S(1)}, u32[]{:S(2)}, u32[]{:S(2)}) collective-permute-start(f32[64,64]{0,1:T(8,128)S(1)} %get-tuple-element.25), channel_id=1, source_target_pairs={{8,0},{16,8},{24,16},{9,1},{17,9},{25,17},{10,2},{18,10},{26,18},{... | collective-permute-start | bytes 49160 | tf_op jit(solution)/shard_map/ppermute | solution.py:27
  139.5 16.3 %collective-permute-start.7 = (f32[64,64]{0,1:T(8,128)S(1)}, f32[64,64]{0,1:T(8,128)S(1)}, u32[]{:S(2)}, u32[]{:S(2)}) collective-permute-start(f32[64,64]{0,1:T(8,128)S(1)} %get-tuple-element.26), channel_id=1, source_target_pairs={{0,8},{8,16},{16,24},{1,9},{9,17},{17,25},{2,10},{10,18},{18,26},{... | collective-permute-start | bytes 49160 | tf_op jit(solution)/shard_map/ppermute | solution.py:27
  202.9 17.7 %collective-permute-start.8 = (f32[1,64,64]{1,2,0:T(8,128)S(1)}, f32[1,64,64]{1,2,0:T(8,128)S(1)}, u32[]{:S(2)}, u32[]{:S(2)}) collective-permute-start(f32[1,64,64]{1,2,0:T(8,128)S(1)} %bitcast.110), channel_id=1, source_target_pairs={{0,8},{8,16},{16,24},{1,9},{9,17},{17,25},{2,10},{10,18},{18,26},{... | collective-permute-start | bytes 49160 | tf_op jit(solution)/shard_map/ppermute | solution.py:18
  204.2 16.4 %collective-permute-start.9 = (f32[1,64,64]{1,2,0:T(8,128)S(1)}, f32[1,64,64]{1,2,0:T(8,128)S(1)}, u32[]{:S(2)}, u32[]{:S(2)}) collective-permute-start(f32[1,64,64]{1,2,0:T(8,128)S(1)} %bitcast.111), channel_id=1, source_target_pairs={{8,0},{16,8},{24,16},{9,1},{17,9},{25,17},{10,2},{18,10},{26,18},{... | collective-permute-start | bytes 49160 | tf_op jit(solution)/shard_map/ppermute | solution.py:19
  212.9 17.8 %collective-permute-start.10 = (f32[64,64]{0,1:T(8,128)S(1)}, f32[64,64]{0,1:T(8,128)S(1)}, u32[]{:S(2)}, u32[]{:S(2)}) collective-permute-start(f32[64,64]{0,1:T(8,128)S(1)} %get-tuple-element.23), channel_id=1, source_target_pairs={{8,0},{16,8},{24,16},{9,1},{17,9},{25,17},{10,2},{18,10},{26,18},{... | collective-permute-start | bytes 49160 | tf_op jit(solution)/shard_map/ppermute | solution.py:27
  214.2 16.5 %collective-permute-start.11 = (f32[64,64]{0,1:T(8,128)S(1)}, f32[64,64]{0,1:T(8,128)S(1)}, u32[]{:S(2)}, u32[]{:S(2)}) collective-permute-start(f32[64,64]{0,1:T(8,128)S(1)} %get-tuple-element.24), channel_id=1, source_target_pairs={{0,8},{8,16},{16,24},{1,9},{9,17},{17,25},{2,10},{10,18},{18,26},{... | collective-permute-start | bytes 49160 | tf_op jit(solution)/shard_map/ppermute | solution.py:27
where the time goes:
time: 278 us; the launch traced here: 276 us
  blocking collectives  119 us (43%)
  matrix products  60.3 us (22%)
  starting transfers between devices  43.4 us (16%)
  waiting for transfers between devices  18.9 us (7%)
  local copies, waits for them, and re-layouts  16.2 us (6%)
  between operations  10.9 us (4%)
  other arithmetic  7.35 us (3%)
    psum x3, blocking collectives, paired_sums(): lax.psum((jnp.sum(current * current), jnp.sum(current * product_image)),...  119 us
    dot_general x3, matrix products, apply_operator(): jnp.einsum('rkij,rkj->ri', couplings, nearby, precision=lax.Precision.HIG...  27 us
    ppermute x6, starting transfers between devices, shifted(): return lax.ppermute(shard, axis, pairs)  22 us
    dot_general x3, matrix products, apply_operator(): jnp.einsum('rkij,ri->rkj', couplings, field, precision=lax.Precision.HIGH...  19.6 us
    all_to_all x1, waiting for transfers between devices, per_device(): lax.all_to_all(tangent_buffer, 'dev', split_axis=0, concat_axis=0, tiled=...  18.9 us
    all_to_all x1, starting transfers between devices, per_device(): lax.all_to_all(row_buffer, 'dev', split_axis=0, concat_axis=0, tiled=True)  7.28 us
    all_to_all x1, starting transfers between devices, per_device(): lax.all_to_all(tangent_buffer, 'dev', split_axis=0, concat_axis=0, tiled=...  6.13 us
  transfers between devices with their start and end apart: 14, of which 1 were waited for; matrix products, arithmetic and copies ran while one was open for 28% of the time, Pallas kernels for 0%

commit v1 on v0

v1 whole, which is shorter than its diff:
```python
import functools

import jax
import jax.numpy as jnp
from jax import lax
from jax.experimental import pallas as pl
from jax.experimental.pallas import tpu as pltpu
from jax.sharding import PartitionSpec as P

BS = 64
ITERS = 3
SHIFT = 4.0
SCALE = 1.0 / 16.0
MESH = pl.DeviceIdType.MESH
F32 = jnp.float32
BF16 = jnp.bfloat16


def prepare(rows, q, couplings_ref, ops_ref, m_ref, b_ref, wide):
    step = couplings_ref.shape[1]
    ks = couplings_ref.shape[0] // rows
    flat = couplings_ref.reshape(rows * ks * step, BS)
    for i in range(step):
        for k in range(0, ks, 2):
            pair = [flat[pl.ds((k + t) * step + i, rows, stride=ks * step), :] for t in range(2)]
            block = jnp.concatenate(pair, axis=0).T
            m_ref[i * BS : (i + 1) * BS, k * rows : (k + 2) * rows] = block

    @pl.when(pl.program_id(0) == 0)
    def _():
        elems = ops_ref.shape[0]
        wide[...] = ops_ref[...].astype(F32).reshape(elems * q, BS)
        for t in range(q // 2):
            pair = [wide[pl.ds(t + h * (q // 2), elems, stride=q), :] for h in range(2)]
            b_ref[t * BS : (t + 1) * BS, :] = jnp.concatenate(pair, axis=0).T


def pieces(x):
    high = x.astype(BF16)
    rest = x - high.astype(F32)
    mid = rest.astype(BF16)
    low = (rest - mid.astype(F32)).astype(BF16)
    return high, mid, low


def dot(a, b, ca, cb):
    return lax.dot_general(a, b, (((ca,), (cb,)), ((), ())), preferred_element_type=F32)


def pick(x, onehot, axis):
    n = x.shape[0]
    out = dot(jnp.concatenate(pieces(x), axis=0), onehot, 1, axis)
    return out[:n] + out[n : 2 * n] + out[2 * n :]


def pick_rows(onehot, x):
    high, mid, low = pieces(x)
    return dot(onehot, high, 1, 1) + dot(onehot, mid, 1, 1) + dot(onehot, low, 1, 1)


def onehot(condition):
    return jnp.where(condition, 1.0, 0.0).astype(BF16)


def iota(shape, dim):
    return lax.broadcasted_iota(jnp.int32, shape, dim)


def halves(x):
    n = x.shape[0] // 2
    return jnp.concatenate([x[:n], x[n:]], axis=1)


def unhalves(x):
    n = x.shape[1] // 2
    return jnp.concatenate([x[:, :n], x[:, n:]], axis=0)


def kernel(
    n_group, n_dev, cap,
    m_ref, b_ref, stiff_ref, owner_ref, slot_ref, cols_ref, mass_ref, rhs_ref,
    sol_ref, res_ref,
    v_wide, y_part, e_part, w_rows,
    table_src, table_dst, field_src, field_dst, back_src, back_dst,
    near_src, near_dst, sum_src, sum_dst, all_src, all_dst,
    dev_send, dev_recv, near_send, near_recv, all_send, all_recv,
):
    g, d = lax.axis_index("group"), lax.axis_index("dev")
    barrier = pltpu.get_barrier_semaphore()
    for s in range(1, n_dev):
        peer = lax.rem(d + s, n_dev)
        pl.semaphore_signal(barrier, inc=1, device_id=(g, peer), device_id_type=MESH)
    for s in range(1, n_group):
        peer = lax.rem(g + s, n_group)
        pl.semaphore_signal(barrier, inc=1, device_id=(peer, d), device_id_type=MESH)

    elems = owner_ref.shape[1]
    rows = rhs_ref.shape[0]
    slots = n_dev * cap
    pairs = cols_ref.shape[1]
    half = cap // 2

    def to_dev(src, dst, phase):
        copies = []
        for s in range(1, n_dev):
            peer = lax.rem(d + s, n_dev)
            copies.append(pltpu.make_async_remote_copy(
                src_ref=src.at[peer], dst_ref=dst.at[d],
                send_sem=dev_send.at[phase, s - 1], recv_sem=dev_recv.at[phase, s - 1],
                device_id=(g, peer), device_id_type=MESH))
        return copies

    def start(copies):
        for copy in copies:
            copy.start()

    def wait(copies):
        for copy in copies:
            copy.wait()

    owner = owner_ref[...]
    device = iota((n_dev, elems), 0)
    member = device == owner
    ahead = onehot(iota((elems, elems), 0) < iota((elems, elems), 1))
    rank = dot(onehot(member), ahead, 1, 0)
    place = jnp.sum(jnp.where(member, rank + (device * cap).astype(F32), 0.0), axis=0, keepdims=True)
    placed = iota((slots, elems), 0) == place.astype(jnp.int32)
    element_at = onehot(placed)
    named = jnp.sum(jnp.where(placed, (slot_ref[...] + 1).astype(F32), 0.0), axis=1, keepdims=True)
    table_src[...] = jnp.broadcast_to(named - 1.0, (slots, 128)).reshape(n_dev, cap, 128)
    cols = cols_ref[...]
    spot = iota((3 * rows, pairs), 0)
    first = jnp.where(g > 0, 0, rows)
    last = jnp.where(g < n_group - 1, 3 * rows, 2 * rows)
    placer = onehot((spot == cols) & (spot >= first) & (spot < last))
    mass = mass_ref[...].T
    stiff = stiff_ref[...]

    pl.semaphore_wait(barrier, n_dev + n_group - 2)
    table = to_dev(table_src, table_dst, 0)
    start(table)
    table_dst[d] = table_src[d]

    up, down = lax.rem(g + 1, n_group), lax.rem(g + n_group - 1, n_group)

    def to_near(step, kind):
        copies = []
        for side, peer in ((0, up), (1, down)):
            src = near_src.at[step, 0] if kind == 0 else near_src.at[step, 1 + side]
            index = step * 4 + kind * 2 + side
            copies.append(pltpu.make_async_remote_copy(
                src_ref=src, dst_ref=near_dst.at[step, kind * 2 + side],
                send_sem=near_send.at[index], recv_sem=near_recv.at[index],
                device_id=(peer, d), device_id_type=MESH))
        return copies

    def apply(v, step, state):
        near_src[step, 0] = halves(v)
        near_field = to_near(step, 0)
        start(near_field)

        def send_field(requested):
            packed = pick_rows(requested, v).reshape(n_dev, 2, half, BS)
            field_src[step] = jnp.concatenate([packed[:, 0], packed[:, 1]], axis=2)
            copies = to_dev(field_src.at[step], field_dst.at[step], 1 + 2 * step)
            start(copies)
            field_dst[step, d] = field_src[step, d]
            return copies

        requested = state
        if step > 0:
            fields = send_field(requested)
        v_wide[...] = jnp.concatenate([v] * (pairs // rows), axis=1)

        def returned(i, total):
            block = m_ref[pl.ds(pl.multiple_of(i * BS, BS), BS), :]
            return total + block * v_wide[pl.ds(i, 1), :]

        back = lax.fori_loop(0, BS, returned, jnp.zeros((BS, pairs), F32), unroll=8)
        spread = pick(back, placer, 1)
        near_src[step, 1] = halves(spread[:, 2 * rows :])
        near_src[step, 2] = halves(spread[:, :rows])
        near_back = to_near(step, 1)
        start(near_back)
        total = spread[:, rows : 2 * rows] + mass * v
        if step == 0:
            wait(table)
            got = table_dst[...].reshape(slots, 128)[:, :rows].astype(jnp.int32)
            requested = onehot(got == iota((slots, rows), 1))
            fields = send_field(requested)

        wait(fields)
        arrived = field_dst[step]
        arrived = jnp.concatenate([arrived[:, :, :BS], arrived[:, :, BS:]], axis=1)
        ve = pick(arrived.reshape(slots, BS).T, element_at, 0)
        ve = jnp.concatenate([ve, ve], axis=1)
        count = stiff.shape[0]
        lanes = 2 * elems
        for t in range(count):
            product = b_ref[t * BS : (t + 1) * BS, :] * ve
            e_part[t * 8 : (t + 1) * 8, :] = jnp.sum(product.reshape(BS // 8, 8, lanes), axis=0)
        strain = e_part[pl.ds(0, count, stride=8), :]
        for s in range(1, 8):
            strain = strain + e_part[pl.ds(s, count, stride=8), :]
        w_rows[...] = strain * stiff
        ye = jnp.zeros((BS, lanes), F32)
        for t in range(count):
            ye = ye + b_ref[t * BS : (t + 1) * BS, :] * w_rows[t : t + 1, :]
        ye = ye[:, :elems] + ye[:, elems:]
        packed = pick_rows(element_at, ye).reshape(n_dev, 2, half, BS)
        back_src[step] = jnp.concatenate([packed[:, 0], packed[:, 1]], axis=2)
        results = to_dev(back_src.at[step], back_dst.at[step], 2 + 2 * step)
        start(results)
        back_dst[step, d] = back_src[step, d]

        wait(near_field)
        extended = jnp.concatenate(
            [unhalves(near_dst[step, 0]), v, unhalves(near_dst[step, 1])], axis=1)
        nearby = pick(extended, placer, 0)

        def cross(i, carry):
            product = m_ref[pl.ds(pl.multiple_of(i * BS, BS), BS), :] * nearby
            part = jnp.sum(product.reshape(BS // 8, 8, pairs), axis=0)
            for h in range(pairs // 128):
                y_part[h, pl.ds(pl.multiple_of(i * 8, 8), 8), :] = part[:, h * 128 : (h + 1) * 128]
            return carry

        lax.fori_loop(0, BS, cross, 0, unroll=8)
        gathered = jnp.zeros((BS, 128), F32)
        for h in range(pairs // 128):
            for s in range(8):
                gathered = gathered + y_part.at[h][pl.ds(s, BS, stride=8), :]
        for t in range(128 // rows):
            total = total + gathered[:, t * rows : (t + 1) * rows]
        wait(near_back)
        total = total + unhalves(near_dst[step, 2]) + unhalves(near_dst[step, 3])
        wait(results)
        arrived = back_dst[step]
        arrived = jnp.concatenate([arrived[:, :, :BS], arrived[:, :, BS:]], axis=1)
        total = total + pick(arrived.reshape(slots, BS).T, requested, 0)
        return total, requested

    basis = [rhs_ref[...].T]
    requested = None
    for step in range(ITERS):
        image, requested = apply(basis[-1], step, requested)
        basis.append((image - SHIFT * basis[-1]) * SCALE)

    entries = [(a, b) for a in range(ITERS + 1) for b in range(a, ITERS + 1)]
    lane = iota((1, 128), 1)
    sums = jnp.zeros((1, 128), F32)
    for index, (a, b) in enumerate(entries):
        column = jnp.sum(basis[a] * basis[b], axis=0, keepdims=True)
        sums = jnp.where(lane == index, jnp.sum(column, axis=1, keepdims=True), sums)
    for s in range(n_dev):
        sum_src[s] = sums
    partial = to_dev(sum_src, sum_dst, 1 + 2 * ITERS)
    start(partial)
    sum_dst[d] = sums
    wait(partial)
    sums = jnp.sum(sum_dst[...], axis=0)
    all_src[...] = sums
    whole = []
    for s in range(1, n_group):
        peer = lax.rem(g + s, n_group)
        whole.append(pltpu.make_async_remote_copy(
            src_ref=all_src, dst_ref=all_dst.at[g],
            send_sem=all_send.at[s - 1], recv_sem=all_recv.at[s - 1],
            device_id=(peer, d), device_id_type=MESH))
    start(whole)
    all_dst[g] = sums
    wait(whole)
    sums = jnp.sum(all_dst[...], axis=0)
    gram = {}
    for index, (a, b) in enumerate(entries):
        value = jnp.broadcast_to(sums[:, index : index + 1], (1, rows))
        gram[a, b] = gram[b, a] = value

    def inner(a, b):
        out = None
        for i, x in enumerate(a):
            line = None
            for j, y in enumerate(b):
                term = y * gram[i, j]
                line = term if line is None else line + term
            out = x * line if out is None else out + x * line
        return out

    def image_of(c):
        out = [SHIFT * x for x in c] + [jnp.zeros_like(c[0])]
        return [out[0]] + [out[k + 1] + c[k] * (1.0 / SCALE) for k in range(len(c))]

    def combine(a, scale, b):
        size = max(len(a), len(b))
        out = []
        for k in range(size):
            if k >= len(b):
                out.append(a[k])
            elif k >= len(a):
                out.append(scale * b[k])
            else:
                out.append(a[k] + scale * b[k])
        return out

    one = jnp.ones((1, rows), F32)
    answer, residual, direction = [], [one], [one]
    norm = gram[0, 0]
    for step in range(ITERS):
        image = image_of(direction)
        alpha = norm / inner(direction, image)
        answer = combine(answer, alpha, direction)
        residual = combine(residual, -alpha, image)
        if step + 1 < ITERS:
            following = inner(residual, residual)
            direction = combine(residual, following / norm, direction)
            norm = following
    sol_ref[...] = sum(c * w for c, w in zip(answer, basis)).T
    res_ref[...] = sum(c * w for c, w in zip(residual, basis)).T


def per_device(n_group, n_dev, elem_ops, elem_stiff, owner, row_slot, couplings, coupling_cols, mass, rhs):
    rows, ks = coupling_cols.shape
    elems, q, _ = elem_ops.shape
    pairs = rows * ks
    cap = max(16, 2 * elems // n_dev)
    slots = n_dev * cap
    steps = 8
    per = BS // steps
    m, b = pl.pallas_call(
        functools.partial(prepare, rows, q),
        grid=(steps,),
        in_specs=[
            pl.BlockSpec((pairs, per, BS), lambda i: (0, i, 0)),
            pl.BlockSpec((elems, q, BS), lambda i: (0, 0, 0)),
        ],
        out_specs=[
            pl.BlockSpec((per * BS, pairs), lambda i: (i, 0)),
            pl.BlockSpec((q // 2 * BS, 2 * elems), lambda i: (0, 0)),
        ],
        out_shape=[
            jax.ShapeDtypeStruct((BS * BS, pairs), F32),
            jax.ShapeDtypeStruct((q // 2 * BS, 2 * elems), F32),
        ],
        scratch_shapes=[pltpu.VMEM((elems * q, BS), F32)],
        compiler_params=pltpu.CompilerParams(vmem_limit_bytes=24 * 2**20),
    )(couplings.reshape(pairs, BS, BS), elem_ops)
    stiff = elem_stiff.T.astype(F32)
    stiff = jnp.concatenate([stiff[: q // 2], stiff[q // 2 :]], axis=1)
    phases = 2 + 2 * ITERS
    vmem = pl.BlockSpec(memory_space=pltpu.VMEM)
    packet = (n_dev, cap // 2, 2 * BS)
    return pl.pallas_call(
        functools.partial(kernel, n_group, n_dev, cap),
        in_specs=[vmem] * 8,
        out_specs=[vmem] * 2,
        out_shape=[jax.ShapeDtypeStruct(rhs.shape, F32)] * 2,
        scratch_shapes=[
            pltpu.VMEM((BS, pairs), F32),
            pltpu.VMEM((pairs // 128, BS * 8, 128), F32),
            pltpu.VMEM((q // 2 * 8, 2 * elems), F32),
            pltpu.VMEM((q // 2, 2 * elems), F32),
            pltpu.VMEM((n_dev, cap, 128), F32),
            pltpu.VMEM((n_dev, cap, 128), F32),
            pltpu.VMEM((ITERS,) + packet, F32),
            pltpu.VMEM((ITERS,) + packet, F32),
            pltpu.VMEM((ITERS,) + packet, F32),
            pltpu.VMEM((ITERS,) + packet, F32),
            pltpu.VMEM((ITERS, 3, BS // 2, 2 * rows), F32),
            pltpu.VMEM((ITERS, 4, BS // 2, 2 * rows), F32),
            pltpu.VMEM((n_dev, 1, 128), F32),
            pltpu.VMEM((n_dev, 1, 128), F32),
            pltpu.VMEM((1, 128), F32),
            pltpu.VMEM((n_group, 1, 128), F32),
            pltpu.SemaphoreType.DMA((phases, n_dev - 1)),
            pltpu.SemaphoreType.DMA((phases, n_dev - 1)),
            pltpu.SemaphoreType.DMA((4 * ITERS,)),
            pltpu.SemaphoreType.DMA((4 * ITERS,)),
            pltpu.SemaphoreType.DMA((n_group - 1,)),
            pltpu.SemaphoreType.DMA((n_group - 1,)),
        ],
        compiler_params=pltpu.CompilerParams(
            collective_id=0, has_side_effects=True, vmem_limit_bytes=32 * 2**20),
    )(m, b, stiff, owner.reshape(1, elems), row_slot.reshape(1, elems),
      coupling_cols.T.reshape(1, pairs), mass, rhs)


def solution(mesh):
    both = ("group", "dev")
    placed = (
        P(both, None, None), P(both, None), P(both, None), P(both),
        P(both, None, None, None), P(both, None), P(both, None), P(both, None),
    )
    return jax.shard_map(
        functools.partial(per_device, mesh.shape["group"], mesh.shape["dev"]),
        mesh=mesh,
        in_specs=placed,
        out_specs=(P(both, None), P(both, None)),
        check_vma=False,
    )
```

time: 278 us -> 63.3 us (0.23)
  blocking collectives: 119 us -> 0 us
  matrix products: 60.3 us -> 0 us
  Pallas kernels: 0 us -> 54.9 us
  starting transfers between devices: 43.4 us -> 0 us
  waiting for transfers between devices: 18.9 us -> 0 us
  between operations: 10.9 us -> 0.72 us
  local copies, waits for them, and re-layouts: 16.2 us -> 6.55 us
  other arithmetic: 7.35 us -> 0.79 us
    psum x3 -> x0, blocking collectives: 119 us -> none  [paired_sums(): lax.psum((jnp.sum(current * current), jnp.sum(current * product_image)),...]
    dot_general x12 -> x0, matrix products: 60.3 us -> none  [the longest x3 27 us: apply_operator(): jnp.einsum('rkij,rkj->ri', couplings, nearby, precision=lax.Precision.HIG...]
    pallas_call x0 -> x2, Pallas kernels: none -> 54.9 us  [the longest x1 47.8 us: per_device(): pl.pallas_call(functools.partial(kernel, n_group, n_dev, cap), in_specs=[...]
    ppermute x12 -> x0, starting transfers between devices: 30 us -> none  [the longest x6 22 us: shifted(): return lax.ppermute(shard, axis, pairs)]
    all_to_all x2 -> x0, waiting for transfers between devices: 18.9 us -> none  [the longest x1 18.9 us: per_device(): lax.all_to_all(tangent_buffer, 'dev', split_axis=0, concat_axis=0, tiled=...]
    all_to_all x2 -> x0, starting transfers between devices: 13.4 us -> none  [the longest x1 7.28 us: per_device(): lax.all_to_all(row_buffer, 'dev', split_axis=0, concat_axis=0, tiled=True)]
    dot_general x6 -> x0, local copies, waits for them, and re-layouts: 4.07 us -> none  [the longest x1 1.88 us: element_tangents(): jnp.einsum('eqi,eq,eqj->eij', values, weights, values, precision=lax.Prec...]
    unnamed x13 -> x14, local copies, waits for them, and re-layouts: 1.8 us -> 5.76 us
  transfers between devices with their start and end apart: 14 -> 0, of which waited for: 1 -> 0; matrix products, arithmetic and copies ran while one was open for 28% -> 0% of each run, Pallas kernels for 0% -> 0%
where the time goes in v1:
time: 63.3 us; the launch traced here: 63 us
  Pallas kernels  54.9 us (87%)
  local copies, waits for them, and re-layouts  6.55 us (10%)
  other arithmetic  0.79 us (1%)
  between operations  0.72 us (1%)
    pallas_call x1, Pallas kernels, per_device(): pl.pallas_call(functools.partial(kernel, n_group, n_dev, cap), in_specs=[...  47.8 us
    pallas_call x1, Pallas kernels, per_device(): pl.pallas_call(functools.partial(prepare, rows, q), grid=(steps,), in_spe...  7.13 us
    unnamed x14, local copies, waits for them, and re-layouts  5.76 us

profile of v1, /device:TPU:0, one launch (start us, length us, event | category | flops | bytes accessed | tf_op | source)
XLA Modules:
  0.0 63.0 jit_solution(11421320410969233174)
XLA Ops:
  0.6 0.0 copy-start.3
  0.6 0.0 copy-start.2
  0.7 0.0 copy-start.5
  0.7 0.0 copy-start.4
  0.7 0.8 %reshape.19.cols_ref = s32[1,256]{1,0:T(1,128)S(1)} reshape(s32[4,64]{1,0:T(4,128)} %bitcast.9) | data formatting | bytes 2048 | tf_op jit(solution)/shard_map/reshape | solution.py:384
  1.5 0.7 %convert_bitcast_fusion = f32[48,64]{1,0:T(8,128)S(1)} fusion(bf16[64,48]{0,1:T(8,128)(2,1)} %param.9), kind=kLoop, calls=%fused_computation | loop fusion | flops 3072 | bytes 18432 | tf_op jit(solution)/shard_map/convert_element_type | solution.py:347
  2.2 0.1 pad_maximum_fusion.stiff_ref
  2.3 0.0 copy-start
  2.3 3.4 %copy-done = f32[64,4,64,64]{3,2,1,0:T(8,128)S(1)} copy-done((f32[64,4,64,64]{3,2,1,0:T(8,128)S(1)}, f32[64,4,64,64]{3,2,1,0:T(8,128)}, u32[]{:S(2)}) %copy-start) | copy-done | bytes 4194328
  5.6 0.0 copy-start.1
  5.6 1.1 %copy-done.1 = bf16[64,48,64]{2,1,0:T(8,128)(2,1)S(1)} copy-done((bf16[64,48,64]{2,1,0:T(8,128)(2,1)S(1)}, bf16[64,48,64]{2,1,0:T(8,128)(2,1)}, u32[]{:S(2)}) %copy-start.1) | copy-done | bytes 393240
  6.8 7.1 %shard_map.95 = (f32[4096,256]{1,0:T(8,128)S(1)}, f32[1536,128]{1,0:T(8,128)S(1)}) custom-call(f32[256,64,64]{2,1,0:T(8,128)S(1)} %bitcast.6, bf16[64,48,64]{2,1,0:T(8,128)(2,1)S(1)} %copy-done.1), custom_call_target="tpu_custom_call" | custom-call | tf_op jit(solution)/shard_map/pallas_call | solution.py:329
  13.9 0.0 copy-done.3
  13.9 0.0 copy-done.2
  13.9 0.0 copy-done.5
  13.9 0.0 copy-done.4
  13.9 47.8 %shard_map.96 = (f32[64,64]{1,0:T(8,128)S(1)}, f32[64,64]{1,0:T(8,128)S(1)}) custom-call(f32[4096,256]{1,0:T(8,128)S(1)} %get-tuple-element.4.m_ref, f32[1536,128]{1,0:T(8,128)S(1)} %get-tuple-element.5.b_ref, f32[24,128]{1,0:T(8,128)S(1)} %pad_maximum_fusion.stiff_ref, s32[1,64]{1,0:T(1,128)S(1)} %bitcast.7, s32[1,64]{1,0:T(1,128)S(1)} %bitcast.8, ...), custom_call_target="tpu_custom_call" | custom-call | tf_op jit(solution)/shard_map/pallas_call | solution.py:352
  61.8 0.6 copy.12
  62.4 0.6 copy.13
  (1 shorter events, 0.0 us)
Async XLA Ops:
  0.6 13.3 %copy-start.3 = (f32[64,64]{1,0:T(8,128)S(1)}, f32[64,64]{1,0:T(8,128)}, u32[]{:S(2)}) copy-start(f32[64,64]{1,0:T(8,128)} %rhs_ref.1) | copy-start | bytes 49156
  0.6 13.3 %copy-start.2 = (f32[64,64]{1,0:T(8,128)S(1)}, f32[64,64]{1,0:T(8,128)}, u32[]{:S(2)}) copy-start(f32[64,64]{1,0:T(8,128)} %mass_ref.1) | copy-start | bytes 49156
  0.7 13.3 %copy-start.5 = (s32[64]{0:T(128)S(1)}, s32[64]{0:T(128)}, u32[]{:S(2)}) copy-start(s32[64]{0:T(128)} %param.11) | copy-start | bytes 772
  0.7 13.3 %copy-start.4 = (s32[64,1]{0,1:T(1,128)S(1)}, s32[64,1]{0,1:T(1,128)}, u32[]{:S(2)}) copy-start(s32[64,1]{0,1:T(1,128)} %param.10) | copy-start | bytes 772
  2.3 3.4 %copy-start = (f32[64,4,64,64]{3,2,1,0:T(8,128)S(1)}, f32[64,4,64,64]{3,2,1,0:T(8,128)}, u32[]{:S(2)}) copy-start(f32[64,4,64,64]{3,2,1,0:T(8,128)} %param.12) | copy-start | bytes 12582916
  5.6 1.1 %copy-start.1 = (bf16[64,48,64]{2,1,0:T(8,128)(2,1)S(1)}, bf16[64,48,64]{2,1,0:T(8,128)(2,1)}, u32[]{:S(2)}) copy-start(bf16[64,48,64]{2,1,0:T(8,128)(2,1)} %ops_ref.1) | copy-start | bytes 1179652

commit v2 on v1

v2 whole, which is shorter than its diff:
```python
import functools

import jax
import jax.numpy as jnp
from jax import lax
from jax.experimental import pallas as pl
from jax.experimental.pallas import tpu as pltpu
from jax.sharding import PartitionSpec as P

BS = 64
ITERS = 3
SHIFT = 4.0
SCALE = 1.0 / 16.0
MESH = pl.DeviceIdType.MESH
F32 = jnp.float32
BF16 = jnp.bfloat16


def pieces(x):
    high = x.astype(BF16)
    rest = x - high.astype(F32)
    mid = rest.astype(BF16)
    low = (rest - mid.astype(F32)).astype(BF16)
    return high, mid, low


def dot(a, b, ca, cb):
    return lax.dot_general(a, b, (((ca,), (cb,)), ((), ())), preferred_element_type=F32)


def pick(x, onehot, axis):
    n = x.shape[0]
    out = dot(jnp.concatenate(pieces(x), axis=0), onehot, 1, axis)
    return out[:n] + out[n : 2 * n] + out[2 * n :]


def onehot(condition):
    return jnp.where(condition, 1.0, 0.0).astype(BF16)


def iota(shape, dim):
    return lax.broadcasted_iota(jnp.int32, shape, dim)


def halves(x):
    n = x.shape[0] // 2
    return jnp.concatenate([x[:n], x[n:]], axis=1)


def unhalves(x):
    n = x.shape[1] // 2
    return jnp.concatenate([x[:, :n], x[:, n:]], axis=0)


def kernel(
    n_group, n_dev, cap,
    couplings_ref, ops_ref, stiff_ref, owner_ref, slot_ref, cols_ref, mass_ref, rhs_ref,
    sol_ref, res_ref,
    raw, ops, wide, m_ref, b_ref, v_wide, y_part, e_part, w_rows,
    table_src, table_dst, elem_src, elem_dst,
    near_src, near_dst, sum_src, sum_dst, all_src, all_dst,
    load_sem, dev_send, dev_recv, near_send, near_recv, all_send, all_recv,
):
    g, d = lax.axis_index("group"), lax.axis_index("dev")
    load_ops = pltpu.make_async_copy(ops_ref, ops, load_sem.at[0])
    load_raw = pltpu.make_async_copy(couplings_ref, raw, load_sem.at[1])
    load_ops.start()
    load_raw.start()
    barrier = pltpu.get_barrier_semaphore()
    for s in range(1, n_dev):
        peer = lax.rem(d + s, n_dev)
        pl.semaphore_signal(barrier, inc=1, device_id=(g, peer), device_id_type=MESH)
    for s in range(1, n_group):
        peer = lax.rem(g + s, n_group)
        pl.semaphore_signal(barrier, inc=1, device_id=(peer, d), device_id_type=MESH)

    elems = owner_ref.shape[1]
    rows = rhs_ref.shape[0]
    slots = n_dev * cap
    ks = cols_ref.shape[0]
    pairs = rows * ks
    q = stiff_ref.shape[0]

    def to_dev(src, dst, phase):
        copies = []
        for s in range(1, n_dev):
            peer = lax.rem(d + s, n_dev)
            copies.append(pltpu.make_async_remote_copy(
                src_ref=src.at[peer], dst_ref=dst.at[d],
                send_sem=dev_send.at[phase, s - 1], recv_sem=dev_recv.at[phase, s - 1],
                device_id=(g, peer), device_id_type=MESH))
        return copies

    def start(copies):
        for copy in copies:
            copy.start()

    def wait(copies):
        for copy in copies:
            copy.wait()

    device = iota((n_dev, elems), 0)
    member = device == owner_ref[...]
    ahead = onehot(iota((elems, elems), 0) < iota((elems, elems), 1))
    rank = dot(onehot(member), ahead, 1, 0)
    place = jnp.sum(jnp.where(member, rank + (device * cap).astype(F32), 0.0), axis=0, keepdims=True)
    placed = iota((slots, elems), 0) == place.astype(jnp.int32)
    element_at = onehot(placed)
    named = jnp.sum(jnp.where(placed, (slot_ref[...] + 1).astype(F32), 0.0), axis=1, keepdims=True)
    stiff = dot(element_at, stiff_ref[...], 1, 1)
    stiff = jnp.concatenate([stiff, jnp.zeros((slots, BS - q), F32)], axis=1)
    sheet = jnp.concatenate([stiff, jnp.broadcast_to(named - 1.0, (slots, BS))], axis=1)
    table_src[...] = sheet.reshape(n_dev, cap, 2 * BS)
    load_ops.wait()
    wide[...] = ops[...].astype(F32).reshape(elems * q, BS)
    for t in range(q // 2):
        pair = [wide[pl.ds(t + h * (q // 2), elems, stride=q), :] for h in range(2)]
        moved = dot(element_at, jnp.concatenate(pair, axis=1).astype(BF16), 1, 0)
        elem_src[:, t * cap : (t + 1) * cap, :] = moved.reshape(n_dev, cap, 2 * BS).astype(BF16)

    pl.semaphore_wait(barrier, n_dev + n_group - 2)
    table = to_dev(table_src, table_dst, 0)
    start(table)
    elements = to_dev(elem_src, elem_dst, 1)
    start(elements)
    table_dst[d] = table_src[d]
    elem_dst[d] = elem_src[d]

    cols = jnp.concatenate([cols_ref[k : k + 1, :] for k in range(ks)], axis=1)
    spot = iota((3 * rows, pairs), 0)
    first = jnp.where(g > 0, 0, rows)
    last = jnp.where(g < n_group - 1, 3 * rows, 2 * rows)
    placer = onehot((spot == cols) & (spot >= first) & (spot < last))
    mass = mass_ref[...].T

    up, down = lax.rem(g + 1, n_group), lax.rem(g + n_group - 1, n_group)

    def to_near(step, kind):
        copies = []
        for side, peer in ((0, up), (1, down)):
            src = near_src.at[step, 0] if kind == 0 else near_src.at[step, 1 + side]
            index = step * 4 + kind * 2 + side
            copies.append(pltpu.make_async_remote_copy(
                src_ref=src, dst_ref=near_dst.at[step, kind * 2 + side],
                send_sem=near_send.at[index], recv_sem=near_recv.at[index],
                device_id=(peer, d), device_id_type=MESH))
        return copies

    def transpose_couplings():
        load_raw.wait()

        def one(i, carry):
            for k in range(0, ks, 2):
                pair = [raw[pl.ds((k + t) * BS + i, rows, stride=ks * BS), :] for t in range(2)]
                block = jnp.concatenate(pair, axis=0).T
                m_ref[pl.ds(pl.multiple_of(i * BS, BS), BS), k * rows : (k + 2) * rows] = block
            return carry

        lax.fori_loop(0, BS, one, 0, unroll=4)

    def take_elements():
        wait(table)
        wait(elements)
        sheet = table_dst[...].reshape(slots, 2 * BS)
        held = onehot(sheet[:, BS:].astype(jnp.int32) == iota((slots, rows), 1))
        for t in range(q // 2):
            block = elem_dst[:, t * cap : (t + 1) * cap, :].astype(F32).reshape(slots, 2 * BS).T
            b_ref[t * BS : (t + 1) * BS, :] = block[:BS]
            b_ref[(t + q // 2) * BS : (t + q // 2 + 1) * BS, :] = block[BS:]
        return held, sheet.T[:q]

    def apply_elements(v, held, stiff):
        ve = pick(v, held, 1)
        for t in range(q):
            product = b_ref[t * BS : (t + 1) * BS, :] * ve
            part = jnp.sum(product.reshape(BS // 8, 8, slots), axis=0)
            for h in range(slots // 128):
                e_part[h, t * 8 : (t + 1) * 8, :] = part[:, h * 128 : (h + 1) * 128]
        for h in range(slots // 128):
            strain = e_part.at[h][pl.ds(0, q, stride=8), :]
            for s in range(1, 8):
                strain = strain + e_part.at[h][pl.ds(s, q, stride=8), :]
            w_rows[:, h * 128 : (h + 1) * 128] = strain * stiff[:, h * 128 : (h + 1) * 128]
        ye = jnp.zeros((BS, slots), F32)
        for t in range(q):
            ye = ye + b_ref[t * BS : (t + 1) * BS, :] * w_rows[t : t + 1, :]
        return pick(ye, held, 0)

    def apply(v, step, state):
        near_src[step, 0] = halves(v)
        near_field = to_near(step, 0)
        start(near_field)
        v_wide[...] = jnp.concatenate([v] * ks, axis=1)
        if step == 0:
            transpose_couplings()

        def returned(i, total):
            block = m_ref[pl.ds(pl.multiple_of(i * BS, BS), BS), :]
            return total + block * v_wide[pl.ds(i, 1), :]

        back = lax.fori_loop(0, BS, returned, jnp.zeros((BS, pairs), F32), unroll=8)
        spread = pick(back, placer, 1)
        near_src[step, 1] = halves(spread[:, 2 * rows :])
        near_src[step, 2] = halves(spread[:, :rows])
        near_back = to_near(step, 1)
        start(near_back)
        total = spread[:, rows : 2 * rows] + mass * v
        if step > 0:
            total = total + apply_elements(v, *state)

        wait(near_field)
        extended = jnp.concatenate(
            [unhalves(near_dst[step, 0]), v, unhalves(near_dst[step, 1])], axis=1)
        nearby = pick(extended, placer, 0)

        def cross(i, carry):
            product = m_ref[pl.ds(pl.multiple_of(i * BS, BS), BS), :] * nearby
            part = jnp.sum(product.reshape(BS // 8, 8, pairs), axis=0)
            for h in range(pairs // 128):
                y_part[h, pl.ds(pl.multiple_of(i * 8, 8), 8), :] = part[:, h * 128 : (h + 1) * 128]
            return carry

        lax.fori_loop(0, BS, cross, 0, unroll=8)
        gathered = jnp.zeros((BS, 128), F32)
        for h in range(pairs // 128):
            for s in range(8):
                gathered = gathered + y_part.at[h][pl.ds(s, BS, stride=8), :]
        for t in range(128 // rows):
            total = total + gathered[:, t * rows : (t + 1) * rows]
        if step == 0:
            state = take_elements()
            total = total + apply_elements(v, *state)
        wait(near_back)
        total = total + unhalves(near_dst[step, 2]) + unhalves(near_dst[step, 3])
        return total, state

    basis = [rhs_ref[...].T]
    state = None
    for step in range(ITERS):
        image, state = apply(basis[-1], step, state)
        basis.append((image - SHIFT * basis[-1]) * SCALE)

    entries = [(a, b) for a in range(ITERS + 1) for b in range(a, ITERS + 1)]
    lane = iota((1, 128), 1)
    sums = jnp.zeros((1, 128), F32)
    for index, (a, b) in enumerate(entries):
        column = jnp.sum(basis[a] * basis[b], axis=0, keepdims=True)
        sums = jnp.where(lane == index, jnp.sum(column, axis=1, keepdims=True), sums)
    for s in range(n_dev):
        sum_src[s] = sums
    partial = to_dev(sum_src, sum_dst, 2)
    start(partial)
    sum_dst[d] = sums
    wait(partial)
    sums = jnp.sum(sum_dst[...], axis=0)
    all_src[...] = sums
    whole = []
    for s in range(1, n_group):
        peer = lax.rem(g + s, n_group)
        whole.append(pltpu.make_async_remote_copy(
            src_ref=all_src, dst_ref=all_dst.at[g],
            send_sem=all_send.at[s - 1], recv_sem=all_recv.at[s - 1],
            device_id=(peer, d), device_id_type=MESH))
    start(whole)
    all_dst[g] = sums
    wait(whole)
    sums = jnp.sum(all_dst[...], axis=0)
    gram = {}
    for index, (a, b) in enumerate(entries):
        value = jnp.broadcast_to(sums[:, index : index + 1], (1, rows))
        gram[a, b] = gram[b, a] = value

    def inner(a, b):
        out = None
        for i, x in enumerate(a):
            line = None
            for j, y in enumerate(b):
                term = y * gram[i, j]
                line = term if line is None else line + term
            out = x * line if out is None else out + x * line
        return out

    def image_of(c):
        out = [SHIFT * x for x in c] + [jnp.zeros_like(c[0])]
        return [out[0]] + [out[k + 1] + c[k] * (1.0 / SCALE) for k in range(len(c))]

    def combine(a, scale, b):
        size = max(len(a), len(b))
        out = []
        for k in range(size):
            if k >= len(b):
                out.append(a[k])
            elif k >= len(a):
                out.append(scale * b[k])
            else:
                out.append(a[k] + scale * b[k])
        return out

    one = jnp.ones((1, rows), F32)
    answer, residual, direction = [], [one], [one]
    norm = gram[0, 0]
    for step in range(ITERS):
        image = image_of(direction)
        alpha = norm / inner(direction, image)
        answer = combine(answer, alpha, direction)
        residual = combine(residual, -alpha, image)
        if step + 1 < ITERS:
            following = inner(residual, residual)
            direction = combine(residual, following / norm, direction)
            norm = following
    sol_ref[...] = sum(c * w for c, w in zip(answer, basis)).T
    res_ref[...] = sum(c * w for c, w in zip(residual, basis)).T


def per_device(n_group, n_dev, elem_ops, elem_stiff, owner, row_slot, couplings, coupling_cols, mass, rhs):
    rows, ks = coupling_cols.shape
    elems, q, _ = elem_ops.shape
    pairs = rows * ks
    cap = max(16, 2 * elems // n_dev)
    slots = n_dev * cap
    vmem = pl.BlockSpec(memory_space=pltpu.VMEM)
    anywhere = pl.BlockSpec(memory_space=pl.ANY)
    packet = (n_dev, q // 2 * cap, 2 * BS)
    return pl.pallas_call(
        functools.partial(kernel, n_group, n_dev, cap),
        in_specs=[anywhere] * 2 + [vmem] * 6,
        out_specs=[vmem] * 2,
        out_shape=[jax.ShapeDtypeStruct(rhs.shape, F32)] * 2,
        scratch_shapes=[
            pltpu.VMEM((pairs * BS, BS), F32),
            pltpu.VMEM((elems, q, BS), BF16),
            pltpu.VMEM((elems * q, BS), F32),
            pltpu.VMEM((BS * BS, pairs), F32),
            pltpu.VMEM((q * BS, slots), F32),
            pltpu.VMEM((BS, pairs), F32),
            pltpu.VMEM((pairs // 128, BS * 8, 128), F32),
            pltpu.VMEM((slots // 128, q * 8, 128), F32),
            pltpu.VMEM((q, slots), F32),
            pltpu.VMEM((n_dev, cap, 2 * BS), F32),
            pltpu.VMEM((n_dev, cap, 2 * BS), F32),
            pltpu.VMEM(packet, BF16),
            pltpu.VMEM(packet, BF16),
            pltpu.VMEM((ITERS, 3, BS // 2, 2 * rows), F32),
            pltpu.VMEM((ITERS, 4, BS // 2, 2 * rows), F32),
            pltpu.VMEM((n_dev, 1, 128), F32),
            pltpu.VMEM((n_dev, 1, 128), F32),
            pltpu.VMEM((1, 128), F32),
            pltpu.VMEM((n_group, 1, 128), F32),
            pltpu.SemaphoreType.DMA((2,)),
            pltpu.SemaphoreType.DMA((3, n_dev - 1)),
            pltpu.SemaphoreType.DMA((3, n_dev - 1)),
            pltpu.SemaphoreType.DMA((4 * ITERS,)),
            pltpu.SemaphoreType.DMA((4 * ITERS,)),
            pltpu.SemaphoreType.DMA((n_group - 1,)),
            pltpu.SemaphoreType.DMA((n_group - 1,)),
        ],
        compiler_params=pltpu.CompilerParams(
            collective_id=0, has_side_effects=True, vmem_limit_bytes=56 * 2**20),
    )(couplings.reshape(pairs * BS, BS), elem_ops, elem_stiff.T, owner.reshape(1, elems),
      row_slot.reshape(1, elems), coupling_cols.T, mass, rhs)


def solution(mesh):
    both = ("group", "dev")
    placed = (
        P(both, None, None), P(both, None), P(both, None), P(both),
        P(both, None, None, None), P(both, None), P(both, None), P(both, None),
    )
    return jax.shard_map(
        functools.partial(per_device, mesh.shape["group"], mesh.shape["dev"]),
        mesh=mesh,
        in_specs=placed,
        out_specs=(P(both, None), P(both, None)),
        check_vma=False,
    )
```

time: 63.3 us -> 46.9 us (0.74)
  Pallas kernels: 54.9 us -> 43.2 us
  local copies, waits for them, and re-layouts: 6.55 us -> 2.75 us
  other arithmetic: 0.79 us -> 0 us
    pallas_call x1 -> x0, Pallas kernels: 7.13 us -> none  [per_device(): pl.pallas_call(functools.partial(prepare, rows, q), grid=(steps,), in_spe...]
    pallas_call x1, Pallas kernels: 47.8 us -> 43.2 us  [per_device(): pl.pallas_call(functools.partial(kernel, n_group, n_dev, cap), in_specs=[...]
    unnamed x14 -> x2, local copies, waits for them, and re-layouts: 5.76 us -> 2.75 us
    reshape x1 -> x0, local copies, waits for them, and re-layouts: 0.79 us -> none  [per_device(): coupling_cols.T.reshape(1, pairs)]
    convert_element_type x1 -> x0, other arithmetic: 0.71 us -> none  [per_device(): stiff = elem_stiff.T.astype(F32)]
where the time goes in v2:
time: 46.9 us; the launch traced here: 46.6 us
  Pallas kernels  43.2 us (92%)
  local copies, waits for them, and re-layouts  2.75 us (6%)
  between operations  0.64 us (1%)
    pallas_call x1, Pallas kernels, per_device(): pl.pallas_call(functools.partial(kernel, n_group, n_dev, cap), in_specs=[...  43.2 us
    unnamed x2, local copies, waits for them, and re-layouts  2.75 us

profile of v2, /device:TPU:0, one launch (start us, length us, event | category | flops | bytes accessed | tf_op | source)
XLA Modules:
  0.0 46.6 jit_solution(10605903360628232900)
XLA Ops:
  0.6 43.2 %shard_map.95 = (f32[64,64]{1,0:T(8,128)}, f32[64,64]{1,0:T(8,128)}) custom-call(f32[16384,64]{1,0:T(8,128)} %bitcast.5, bf16[64,48,64]{2,1,0:T(8,128)(2,1)} %ops_ref.1, bf16[48,64]{1,0:T(8,128)(2,1)} %bitcast.6, s32[1,64]{1,0:T(1,128)} %bitcast.8, s32[1,64]{1,0:T(1,128)} %bitcast.9, s32[4,64]{1,0:T(4,128)} %bitcast.7, f32[64,64]{1,0:T(8,128)} %mass_ref.1, ...), custom_call_target="tpu_custom_call" | custom-call | tf_op jit(solution)/shard_map/pallas_call | solution.py:324
  43.8 1.4 %copy.12 = f32[64,64]{1,0:T(8,128)} copy(f32[64,64]{1,0:T(8,128)} %get-tuple-element.4) | data formatting | bytes 32768
  45.2 1.4 %copy.13 = f32[64,64]{1,0:T(8,128)} copy(f32[64,64]{1,0:T(8,128)} %get-tuple-element.5) | data formatting | bytes 32768
